TPU v7x, 32 devices: a whole 2x2x4 slice. The times are simulated.
32 devices in a mesh: replica: 4 (over z), fsdp: 8 (over y, x, core).
Axes of the slice: x: 2, y: 2, z: 4, core: 2. Of those that a mesh axis runs over, the one named last changes fastest.
Arguments:
- frames: bfloat16 [2, 8192, 3072], P(None, ('replica', 'fsdp')), may hold values from -0.3984375 to 0.3984375
- out_weight: bfloat16 [3072, 2048], P('fsdp'), may hold values from -200 to 200
- align: int32 [2, 8192], P(None, ('replica', 'fsdp')), may hold values from 0 to 2047
- lengths: int32 [2, 32], P(None, ('replica', 'fsdp')), may hold values from 64 to 256, as said below
- deltas: float32 [16, 4, 524288], P(None, 'replica', 'fsdp'), may hold values from -6 to 6
- momentum: float32 [16, 524288], P(None, 'fsdp'), may hold values from -6 to 6
- fragment: int32 [1], replicated, may hold values from 0 to 15
Outputs:
- weight_grad: bfloat16 [4, 3072, 2048], P('replica', 'fsdp')
- frame_grad: bfloat16 [2, 8192, 3072], P(None, ('replica', 'fsdp'))
- loss: float32 [4], P('replica')
- new_momentum: float32 [524288], P('fsdp')
- outer_step: float32 [524288], P('fsdp')
Inputs may be any that keep to these rules, and one draw needn't show every extreme that they name: `lengths`: one slot of every micro-batch holds a full utterance of 256 frames.
All inputs are finite; a program needn't handle non-finite values.
Results may differ from a plain program's by a relative error of at most 0.017.
The roundings to bfloat16 on the way count: a program that leaves them out, or rounds other values in their place, can miss the bound.
Values may be sent and summed in bfloat16 or wider, within the bound.
A program may use at most 128 MiB of HBM per device.

v0:
```python
import jax
import jax.numpy as jnp
from jax import lax
from jax.sharding import PartitionSpec as P


def per_device(frames, out_weight, align, lengths, deltas, momentum, fragment):
    chosen = lax.dynamic_index_in_dim(deltas, fragment[0], 0, keepdims=False)[0]
    previous = lax.dynamic_index_in_dim(momentum, fragment[0], 0, keepdims=False)
    groups = lax.axis_size("replica")
    average = lax.psum(chosen.astype(jnp.bfloat16), "replica").astype(jnp.float32) / groups
    new_momentum = 0.9 * previous + average
    outer_step = average + 0.9 * new_momentum
    weight = lax.all_gather(out_weight, "fsdp", axis=0, tiled=True)
    micro, slots, width_d = frames.shape
    count_rows = micro * slots
    block = frames.reshape(count_rows, width_d).astype(jnp.float32)
    center = block - jnp.mean(block, axis=1, keepdims=True)
    inv_std = lax.rsqrt(jnp.mean(center * center, axis=1, keepdims=True) + 1e-05)
    normed = center * inv_std
    normed_b = normed.astype(jnp.bfloat16)
    logits = jnp.dot(normed_b, weight, preferred_element_type=jnp.float32)
    logp = jax.nn.log_softmax(logits, axis=1)
    states = weight.shape[1]
    labels = align.reshape(count_rows)
    onehot = (labels[:, None] == jnp.arange(states, dtype=jnp.int32)[None, :]).astype(jnp.float32)
    position = jnp.arange(slots, dtype=jnp.int32)
    valid = (position[None, :] < lengths).astype(jnp.float32).reshape(count_rows)
    picked = jnp.sum(onehot * logp, axis=1)
    local_loss = -jnp.sum(valid * picked)
    total_loss = lax.psum(local_loss, "fsdp")
    loss = (total_loss / (count_rows * lax.axis_size("fsdp"))).reshape(1)
    dlogits = (valid[:, None] * (jnp.exp(logp) - onehot)).astype(jnp.bfloat16)
    summed = lax.psum_scatter(
        lax.dot_general(
            normed_b, dlogits, (((0,), (0,)), ((), ())), preferred_element_type=jnp.float32
        ).astype(jnp.bfloat16),
        "fsdp",
        scatter_dimension=0,
        tiled=True,
    )
    dnormed = lax.dot_general(
        dlogits, weight, (((1,), (1,)), ((), ())), preferred_element_type=jnp.float32
    )
    mean_grad = jnp.mean(dnormed, axis=1, keepdims=True)
    mean_proj = jnp.mean(dnormed * normed, axis=1, keepdims=True)
    frame_grad = (
        (inv_std * (dnormed - mean_grad - normed * mean_proj))
        .astype(jnp.bfloat16)
        .reshape(micro, slots, width_d)
    )
    weight_grad = summed.reshape(1, out_weight.shape[0], states)
    return (weight_grad, frame_grad, loss, new_momentum, outer_step)


def solution(mesh):
    return jax.shard_map(
        per_device,
        mesh=mesh,
        in_specs=(
            P(None, ("replica", "fsdp"), None),
            P("fsdp", None),
            P(None, ("replica", "fsdp")),
            P(None, ("replica", "fsdp")),
            P(None, "replica", "fsdp"),
            P(None, "fsdp"),
            P(),
        ),
        out_specs=(
            P("replica", "fsdp", None),
            P(None, ("replica", "fsdp"), None),
            P("replica"),
            P("fsdp"),
            P("fsdp"),
        ),
        check_vma=False,
    )
```

profile of v0, /device:TPU:0, one launch (start us, length us, event | category | flops | bytes accessed | tf_op | source)
XLA Modules:
  0.0 211.4 jit_solution(12797608060335425358)
XLA Ops:
  8.0 0.0 copy-start
  8.0 0.0 copy-start.4
  8.0 0.0 copy-start.3
  8.0 0.0 all-gather.2.cloned.1.call-start
  8.1 0.7 all-gather.2.cloned.1.call-update
  8.8 0.0 all-reduce.2.cloned.1.call-start
  9.6 2.3 %convert_reduce_fusion.1 = bf16[65536]{0:T(1024)(128)(2,1)} fusion(f32[16,1,65536]{2,1,0:T(1,128)} %param.11, s32[]{:T(128)S(6)} %select_n.6), kind=kLoop, calls=%fused_computation.15 | loop fusion | bytes 262148 | tf_op jit(solution)/shard_map/convert_element_type | solution.py:11
  11.9 0.0 all-reduce.2.cloned.1.call-update
  11.9 0.0 reduce-scatter.2.cloned.1.call-start
  12.0 2.4 %convert_reduce_fusion = f32[2,256]{1,0:T(2,128)S(1)} fusion(bf16[2,256,3072]{2,1,0:T(8,128)(2,1)} %param.7), kind=kLoop, calls=%fused_computation.7 | loop fusion | flops 3145216 | bytes 3147776 | tf_op jit(solution)/shard_map/reduce_sum | solution.py:18
  14.4 0.0 copy-done
  14.4 1.0 multiply_reduce_fusion.1
  15.4 0.0 copy-done.4
  15.4 0.1 iota_compare_fusion.1
  15.5 0.0 copy-done.3
  15.5 3.1 %fusion.1 = bf16[512,3072]{1,0:T(8,128)(2,1)} fusion(bf16[2,256,3072]{2,1,0:T(8,128)(2,1)S(1)} %copy-done, f32[512]{0:T(512)S(1)} %bitcast.33, f32[512]{0:T(512)S(1)} %bitcast.36), kind=kLoop, calls=%fused_computation.6 | loop fusion | flops 6291456 | bytes 6295552 | tf_op jit(solution)/shard_map/convert_element_type | solution.py:21
  18.5 67.1 %all-gather.2.cloned.1.call-done = bf16[3072,2048]{1,0:T(8,128)(2,1)} async-done(((bf16[384,2048]{1,0:T(8,128)(2,1)}), bf16[3072,2048]{1,0:T(8,128)(2,1)}) %all-gather.2.cloned.1.call-update) | async-done | bytes 12582928 | tf_op jit(solution)/shard_map/all_gather | solution.py:14
  85.6 10.7 %fusion.7 = (f32[512]{0:T(512)S(1)}, f32[512,2048]{1,0:T(8,128)S(1)}) fusion(bf16[512,3072]{1,0:T(8,128)(2,1)} %fusion.1, bf16[3072,2048]{1,0:T(8,128)(2,1)} %all-gather.2.cloned.1.call-done), kind=kOutput, calls=%fused_computation.26 | convolution fusion | flops 6443499008 | bytes 19924992 | tf_op jit(solution)/shard_map/dot_general | solution.py:22
  96.3 0.0 copy-start.1
  96.3 0.0 copy-start.2
  96.4 0.7 exponential_reduce_fusion
  97.1 1.4 copy-done.1
  98.5 1.3 copy-done.2
  99.8 10.5 %convolution_convert_fusion = bf16[3072,2048]{1,0:T(8,128)(2,1)} fusion(bf16[512,3072]{1,0:T(8,128)(2,1)S(1)} %copy-done.2, f32[512,2048]{1,0:T(8,128)S(1)} %get-tuple-element.12, s32[512]{0:T(512)S(1)} %bitcast.39, f32[512]{0:T(512)S(1)} %log.9, f32[512]{0:T(512)S(1)} %get-tuple-element.11, f32[512]{0:T(512)S(1)} %convert_element_type.47), kind=kOutput, calls=%fused_computation | convolution fusion | flops 6456082432 | bytes 19931136 | tf_op jit(solution)/shard_map/dot_general | solution.py:35
  110.2 0.0 reduce-scatter.2.cloned.1.call-update
  110.2 1.9 dynamic-slice_multiply_fusion
  112.1 3.1 %select_reduce_fusion = f32[512]{0:T(512)S(1)} fusion(f32[512,2048]{1,0:T(8,128)} %copy-done.1, s32[512]{0:T(512)S(1)} %bitcast.40, f32[512]{0:T(512)S(1)} %log.9, f32[512]{0:T(512)S(1)} %get-tuple-element.11), kind=kLoop, calls=%fused_computation.8 | loop fusion | flops 5242368 | bytes 4202496 | tf_op jit(solution)/shard_map/reduce_sum | solution.py:29
  115.2 0.6 select_reduce_fusion.1
  116.5 0.0 all-reduce.2.cloned.1.call-done
  116.5 1.7 multiply_add_fusion
  118.3 13.8 %psum.14 = f32[]{:T(128)} all-reduce(f32[]{:T(128)S(6)} %neg.3), channel_id=1, replica_groups=mesh['replica'=4,'fsdp'=8] {'fsdp'}, use_global_device_ids=true, to_apply=%region_9.10 | all-reduce | flops 1 | bytes 8 | tf_op jit(solution)/shard_map/psum | solution.py:31
  132.8 14.9 %fusion.5 = (f32[512]{0:T(512)S(1)}, f32[512]{0:T(512)S(1)}, f32[512,3072]{1,0:T(8,128)}) fusion(f32[512]{0:T(512)S(1)} %bitcast.34, f32[512]{0:T(512)S(1)} %bitcast.37, bf16[2,256,3072]{2,1,0:T(8,128)(2,1)S(1)} %copy-done, bf16[3072,2048]{1,0:T(8,128)(2,1)} %all-gather.2.cloned.1.call-done, f32[512,2048]{1,0:T(8,128)} %copy-done.1, s32[512]{0:T(512)S(1)} %bitcast.41, ...), kind=kOutput, calls=%fused_computation.25 | convolution fusion | flops 6459227136 | bytes 26230784 | tf_op jit(solution)/shard_map/dot_general | solution.py:42
  147.7 5.8 %multiply_convert_fusion = bf16[512,3072]{1,0:T(8,128)(2,1)} fusion(f32[512,3072]{1,0:T(8,128)} %get-tuple-element.13, bf16[2,256,3072]{2,1,0:T(8,128)(2,1)S(1)} %copy-done, f32[512]{0:T(512)S(1)} %get-tuple-element.14, f32[512]{0:T(512)S(1)} %get-tuple-element.15, f32[512]{0:T(512)S(1)} %bitcast.35, f32[512]{0:T(512)S(1)} %bitcast.38), kind=kLoop, calls=%fused_computation.3 | loop fusion | flops 12582912 | bytes 12591104 | tf_op jit(solution)/shard_map/convert_element_type | solution.py:49
  153.5 49.3 %reduce-scatter.2.cloned.1.call-done = bf16[384,2048]{1,0:T(8,128)(2,1)} async-done(((bf16[3072,2048]{1,0:T(8,128)(2,1)}), bf16[384,2048]{1,0:T(8,128)(2,1)}) %reduce-scatter.2.cloned.1.call-update) | async-done | bytes 1572880 | tf_op jit(solution)/shard_map/reduce_scatter | solution.py:34
  (9 shorter events, 0.1 us)
Async XLA Ops:
  8.0 6.4 %copy-start = (bf16[2,256,3072]{2,1,0:T(8,128)(2,1)S(1)}, bf16[2,256,3072]{2,1,0:T(8,128)(2,1)}, u32[]{:S(2)}) copy-start(bf16[2,256,3072]{2,1,0:T(8,128)(2,1)} %param.7) | copy-start | bytes 9437188
  8.0 7.4 %copy-start.4 = (s32[2,1]{0,1:T(1,128)S(1)}, s32[2,1]{0,1:T(1,128)}, u32[]{:S(2)}) copy-start(s32[2,1]{0,1:T(1,128)} %param.10) | copy-start | bytes 28
  8.0 7.5 %copy-start.3 = (s32[2,256]{1,0:T(2,128)S(1)}, s32[2,256]{1,0:T(2,128)}, u32[]{:S(2)}) copy-start(s32[2,256]{1,0:T(2,128)} %param.9) | copy-start | bytes 6148
  8.0 77.6 %all-gather.2.cloned.1.call-start = ((), (), s32[]{:S(2)}) async-start(), calls=%async_computation.1 | async-start | bytes 14155776 | tf_op jit(solution)/shard_map/all_gather | solution.py:14
  8.8 107.8 %all-reduce.2.cloned.1.call-start = ((), (), s32[]{:S(2)}) async-start(), calls=%async_computation.3 | async-start | bytes 262144 | tf_op jit(solution)/shard_map/psum | solution.py:11
  11.9 190.8 %reduce-scatter.2.cloned.1.call-start = ((), (), s32[]{:S(2)}) async-start(), calls=%async_computation.2 | async-start | bytes 14155776 | tf_op jit(solution)/shard_map/reduce_scatter | solution.py:34
  96.3 2.1 %copy-start.1 = (f32[512,2048]{1,0:T(8,128)}, f32[512,2048]{1,0:T(8,128)S(1)}, u32[]{:S(2)}) copy-start(f32[512,2048]{1,0:T(8,128)S(1)} %get-tuple-element.12) | copy-start | bytes 12582916
  96.3 3.4 %copy-start.2 = (bf16[512,3072]{1,0:T(8,128)(2,1)S(1)}, bf16[512,3072]{1,0:T(8,128)(2,1)}, u32[]{:S(2)}) copy-start(bf16[512,3072]{1,0:T(8,128)(2,1)} %fusion.1) | copy-start | bytes 9437188
Sparse Core Ops, SparseCore 0:
  10.8 74.8 all-gather.1
  110.4 92.3 reduce-scatter.1
Sparse Core Ops, SparseCore 1:
  12.1 36.9 all-reduce.1
where the time goes:
time: 212 us; the launch traced here: 211 us
  waiting for transfers between devices  117 us (55%)
  matrix products  36.1 us (17%)
  other arithmetic  20.4 us (10%)
  between operations  18.8 us (9%)
  blocking collectives  13.8 us (7%)
  local copies, waits for them, and re-layouts  5.02 us (2%)
    all_gather x1, waiting for transfers between devices, per_device(): weight = lax.all_gather(out_weight, 'fsdp', axis=0, tiled=True)  67.1 us
    reduce_scatter x1, waiting for transfers between devices, per_device(): lax.psum_scatter(lax.dot_general(normed_b, dlogits, (((0,), (0,)), ((), (...  49.3 us
    dot_general x1, matrix products, per_device(): lax.dot_general(dlogits, weight, (((1,), (1,)), ((), ())), preferred_elem...  14.9 us
    psum x1, blocking collectives, per_device(): total_loss = lax.psum(local_loss, 'fsdp')  13.8 us
    dot_general x1, matrix products, per_device(): logits = jnp.dot(normed_b, weight, preferred_element_type=jnp.float32)  10.7 us
    dot_general x1, matrix products, per_device(): lax.dot_general(normed_b, dlogits, (((0,), (0,)), ((), ())), preferred_el...  10.5 us
    convert_element_type x1, other arithmetic, per_device(): frame_grad = (inv_std * (dnormed - mean_grad - normed * mean_proj)).astyp...  5.84 us
  transfers between devices with their start and end apart: 3, of which 2 were waited for; matrix products, arithmetic and copies ran while one was open for 28% of the time, Pallas kernels for 0%

commit v1 on v0

v1 whole, which is shorter than its diff:
```python
import functools

import jax
import jax.numpy as jnp
from jax import lax
from jax.experimental import pallas as pl
from jax.experimental.pallas import tpu as pltpu
from jax.sharding import PartitionSpec as P

MESH = pl.DeviceIdType.MESH
F32 = jnp.float32
BF16 = jnp.bfloat16


def flip(index, mask):
    bit = 1
    out = index
    while bit <= mask:
        if mask & bit:
            out = out + bit * (1 - 2 * ((index // bit) % 2))
        bit *= 2
    return out


def popcount(value):
    return bin(value).count("1")


def plan(links):
    chips = 2**links
    ids = {}

    def new(key):
        ids[key] = len(ids)

    new(("own_core",))
    for p in range(links):
        for m in range(1, chips):
            new(("gather", p, m))
            new(("gather_core", p, m))
    for m in range(chips):
        new(("term_core", m))
    for p in range(links):
        for s in range(links):
            for m in range(chips):
                if all(not m & order(links, p)[t] for t in range(s + 1)):
                    new(("reduce", p, s, m))
    return ids


def order(links, p):
    return [1 << ((p + s) % links) for s in range(links)]


def kernel(n, groups, links, ids, slots, frames_hbm, w_hbm, lab_ref, mine_ref, prev_ref,
           wg_hbm, fg_hbm, loss_ref, mom_ref, step_ref,
           fbuf, inv_ref, nb, nbt, wbuf, logits, dl, dn, tb, crecv, rx, wgbuf,
           dsend, drecv, losssend, lossrecv,
           send, recv, small_send, small_recv, local):
    me = lax.axis_index("fsdp")
    group = lax.axis_index("replica")
    core = me % 2
    other = 1 - core
    chip = me // 2
    chips = 2**links
    rows, width = fbuf.shape
    depth, states = w_hbm.shape
    part = depth // links
    both = 2 * depth
    ntile = 256

    def peer(bit):
        return {"fsdp": flip(me, 2 * bit)}

    sibling = {"fsdp": flip(me, 1)}

    def rdma(key, src, dst, where):
        i = ids[key]
        return pltpu.make_async_remote_copy(
            src_ref=src, dst_ref=dst, send_sem=send.at[i], recv_sem=recv.at[i],
            device_id=where, device_id_type=MESH)

    frames_in = pltpu.make_async_copy(frames_hbm, fbuf, local.at[0])
    frames_in.start()
    own_in = pltpu.make_async_copy(w_hbm, wbuf.at[0, core], local.at[1])
    own_in.start()

    barrier = pltpu.get_barrier_semaphore()
    for k in range(1, n):
        pl.semaphore_signal(barrier, inc=1, device_id={"fsdp": flip(me, k)}, device_id_type=MESH)
    for k in range(1, groups):
        pl.semaphore_signal(
            barrier, inc=1, device_id={"replica": lax.rem(group + k, groups)}, device_id_type=MESH)
    pl.semaphore_wait(barrier, n - 1 + groups - 1)

    started = []

    def go(copy):
        copy.start()
        started.append(copy)

    def span(p):
        return pl.ds(p * part, part)

    def gather_copy(p, s, m):
        bit = order(links, p)[s]
        src = w_hbm.at[span(p)] if m == 0 else wbuf.at[m, core, span(p)]
        return rdma(("gather", p, m | bit), src, wbuf.at[m | bit, core, span(p)], peer(bit))

    def gather_core_copy(p, m):
        return rdma(("gather_core", p, m), wbuf.at[m, core, span(p)],
                    wbuf.at[m, core, span(p)], sibling)

    for s in range(links):
        for p in range(links):
            go(gather_copy(p, s, 0))
    own_core = rdma(("own_core",), w_hbm, wbuf.at[0, core], sibling)
    go(own_core)

    dsend[...] = mine_ref[...].astype(BF16)
    small = []
    for k in range(1, groups):
        copy = pltpu.make_async_remote_copy(
            src_ref=dsend, dst_ref=drecv.at[k - 1], send_sem=small_send.at[k - 1],
            recv_sem=small_recv.at[k - 1],
            device_id={"replica": lax.rem(group + k, groups)}, device_id_type=MESH)
        copy.start()
        small.append(copy)

    frames_in.wait()

    tile = 16

    def norm_tile(i, carry):
        r = pl.ds(pl.multiple_of(i * tile, tile), tile)
        x = fbuf[r, :].astype(F32)
        center = x - jnp.mean(x, axis=1, keepdims=True)
        inv = lax.rsqrt(jnp.mean(center * center, axis=1, keepdims=True) + 1e-05)
        nb[r, :] = (center * inv).astype(BF16)
        inv_ref[r, :] = inv
        return carry

    lax.fori_loop(0, rows // tile, norm_tile, 0)

    def transpose_tile(i, carry):
        c = pl.ds(pl.multiple_of(i * ntile, ntile), ntile)
        nbt[c, :] = nb[:, c].T
        return carry

    def columns(m):
        return pl.ds(pl.multiple_of(flip(chip, m) * both, both), both)

    def logits_chip(m, first):
        lhs = nb[:, columns(m)]

        def body(i, carry):
            c = pl.ds(pl.multiple_of(i * ntile, ntile), ntile)
            w = wbuf[m, :, :, c].reshape(both, ntile)
            out = jnp.dot(lhs, w, preferred_element_type=F32)
            if first:
                logits[:, c] = out
            else:
                logits[:, c] += out
            return carry

        lax.fori_loop(0, states // ntile, body, 0)

    arrivals = []
    for m in range(1, chips):
        for p in range(links):
            bits = order(links, p)
            last = max(s for s in range(links) if m & bits[s])
            arrivals.append((popcount(m), last, p, m))
    arrivals.sort()

    def arrive(last, p, m):
        bits = order(links, p)
        gather_copy(p, last, m & ~bits[last]).wait_recv()
        for s in range(last + 1, links):
            go(gather_copy(p, s, m))
        go(gather_core_copy(p, m))

    done = set()
    logged = [False]

    def ready_dots():
        for m in range(1, chips):
            if m not in done and all((p, m) in seen for p in range(links)):
                done.add(m)
                for p in range(links):
                    gather_core_copy(p, m).wait_recv()
                logits_chip(m, False)

    seen = set()
    for index, (_, last, p, m) in enumerate(arrivals):
        arrive(last, p, m)
        seen.add((p, m))
        if index == links - 1:
            lax.fori_loop(0, width // ntile, transpose_tile, 0)
            own_in.wait()
            own_core.wait_recv()
            logits_chip(0, True)
        if index >= links - 1 and (index + 1) % links == 0:
            ready_dots()
    ready_dots()

    def softmax_tile(i, total):
        r = pl.ds(pl.multiple_of(i * tile, tile), tile)
        z = logits[r, :]
        lab = lab_ref[r, :]
        top = jnp.max(z, axis=1, keepdims=True)
        e = jnp.exp(z - top)
        norm = jnp.sum(e, axis=1, keepdims=True)
        valid = (lab >= 0).astype(F32)
        hit = lax.broadcasted_iota(jnp.int32, (tile, states), 1) == lab
        picked = jnp.sum(jnp.where(hit, z, 0.0), axis=1, keepdims=True)
        scale = valid / norm
        d = e * scale
        dl[r, :] = jnp.where(hit, d - 1.0, d).astype(BF16)
        return total + valid * (top + jnp.log(norm) - picked)

    total = lax.fori_loop(0, rows // tile, softmax_tile, jnp.zeros((tile, 1), F32))

    slot_of = slots

    def term(m):
        lhs = nbt[columns(m), :]

        def body(i, carry):
            c = pl.ds(pl.multiple_of(i * ntile, ntile), ntile)
            out = jnp.dot(lhs, dl[:, c], preferred_element_type=F32).astype(BF16)
            tb[m, :, :, c] = out.reshape(2, depth, ntile)
            return carry

        lax.fori_loop(0, states // ntile, body, 0)

    def term_copy(m):
        return rdma(("term_core", m), tb.at[m, other], crecv.at[m], sibling)

    def reduce_copy(p, s, m):
        bit = order(links, p)[s]
        there = m & ~bit
        return rdma(("reduce", p, s, there), tb.at[m, core, span(p)],
                    rx.at[slot_of[(p, s, there)]], peer(bit))

    add_tile = 32

    def add_core(m):
        def body(i, carry):
            r = pl.ds(pl.multiple_of(i * add_tile, add_tile), add_tile)
            tb[m, core, r, :] = (tb[m, core, r, :].astype(F32) + crecv[m, r, :].astype(F32)).astype(BF16)
            return carry

        lax.fori_loop(0, depth // add_tile, body, 0)

    def finish_core(m):
        term_copy(m).wait_recv()
        add_core(m)
        for p in range(links):
            if m & order(links, p)[0]:
                go(reduce_copy(p, 0, m))

    masks = sorted(range(chips), key=lambda m: (-popcount(m), m))
    for index, m in enumerate(masks):
        term(m)
        go(term_copy(m))
        if index:
            finish_core(masks[index - 1])
    finish_core(masks[-1])

    losssend[...] = jnp.broadcast_to(jnp.sum(total, axis=0, keepdims=True), losssend.shape)
    losses = []
    for k in range(1, n):
        copy = pltpu.make_async_remote_copy(
            src_ref=losssend, dst_ref=lossrecv.at[k - 1],
            send_sem=small_send.at[groups - 2 + k], recv_sem=small_recv.at[groups - 2 + k],
            device_id={"fsdp": flip(me, k)}, device_id_type=MESH)
        copy.start()
        losses.append(copy)

    def dnormed(m):
        w = wbuf[m].reshape(both, states)
        half = rows // 2

        def body(i, carry):
            r = pl.ds(pl.multiple_of(i * half, half), half)
            dn[r, columns(m)] = lax.dot_general(
                dl[r, :], w, (((1,), (1,)), ((), ())), preferred_element_type=F32)
            return carry

        lax.fori_loop(0, 2, body, 0)

    for m in masks:
        dnormed(m)

    def add_received(p, s, m):
        def body(i, carry):
            r = pl.multiple_of(i * add_tile, add_tile)
            here = pl.ds(p * part + r, add_tile)
            value = tb[m, core, here, :].astype(F32)
            for t in range(s):
                value = value + rx[slot_of[(p, t, m)], pl.ds(r, add_tile), :].astype(F32)
            if m == 0:
                wgbuf[here, :] = value.astype(BF16)
            else:
                tb[m, core, here, :] = value.astype(BF16)
            return carry

        lax.fori_loop(0, part // add_tile, body, 0)

    def reduce_wait(p, s, m):
        bit = order(links, p)[s]
        reduce_copy(p, s, m | bit).wait_recv()

    waited = set()

    def need(p, s, m):
        for t in range(s):
            if (p, t, m) not in waited:
                waited.add((p, t, m))
                reduce_wait(p, t, m)

    for s in range(1, links):
        for p in range(links):
            bits = order(links, p)
            for m in masks:
                if m & bits[s] and all(not m & bits[t] for t in range(s)):
                    need(p, s, m)
                    add_received(p, s, m)
                    go(reduce_copy(p, s, m))

    def grad_tile(i, carry):
        r = pl.ds(pl.multiple_of(i * tile, tile), tile)
        d = dn[r, :]
        x = nb[r, :].astype(F32)
        mean_grad = jnp.mean(d, axis=1, keepdims=True)
        mean_proj = jnp.mean(d * x, axis=1, keepdims=True)
        fbuf[r, :] = (inv_ref[r, :] * (d - mean_grad - x * mean_proj)).astype(BF16)
        return carry

    lax.fori_loop(0, rows // tile, grad_tile, 0)
    frames_out = pltpu.make_async_copy(fbuf, fg_hbm, local.at[0])
    frames_out.start()

    for copy in small:
        copy.wait_recv()
    average = mine_ref[...].astype(BF16).astype(F32)
    for k in range(1, groups):
        average = average + drecv[k - 1].astype(F32)
    average = average * (1.0 / groups)
    momentum = 0.9 * prev_ref[...] + average
    mom_ref[...] = momentum
    step_ref[...] = average + 0.9 * momentum

    for copy in losses:
        copy.wait_recv()
    value = losssend[...]
    for k in range(1, n):
        value = value + lossrecv[k - 1]
    loss_ref[...] = value * (1.0 / (rows * n))

    for p in range(links):
        need(p, links, 0)
        add_received(p, links, 0)
    grad_out = pltpu.make_async_copy(wgbuf, wg_hbm, local.at[1])
    grad_out.start()
    for copy in started + small + losses:
        copy.wait_send()
    frames_out.wait()
    grad_out.wait()


def per_device(frames, out_weight, align, lengths, deltas, momentum, fragment):
    n = lax.axis_size("fsdp")
    groups = lax.axis_size("replica")
    links = n.bit_length() - 2
    chips = 2**links
    micro, per, width = frames.shape
    rows = micro * per
    depth, states = out_weight.shape
    part = depth // links
    chosen = lax.dynamic_index_in_dim(deltas, fragment[0], 0, keepdims=False)[0]
    previous = lax.dynamic_index_in_dim(momentum, fragment[0], 0, keepdims=False)
    entries = chosen.shape[0]
    lanes = (entries // 128, 128)
    position = jnp.arange(per, dtype=jnp.int32)
    lab = jnp.where(position[None, :] < lengths, align, -1).reshape(rows, 1)

    ids = plan(links)
    slots = {}
    for key in ids:
        if key[0] == "reduce":
            slots[key[1:]] = len(slots)
    nsmall = groups - 1 + n - 1
    hbm = pl.BlockSpec(memory_space=pl.ANY)
    vmem = pl.BlockSpec(memory_space=pltpu.VMEM)
    flops = 6 * rows * width * states
    wg, fg, loss, mom, step = pl.pallas_call(
        functools.partial(kernel, n, groups, links, ids, slots),
        out_shape=(
            jax.ShapeDtypeStruct((depth, states), BF16),
            jax.ShapeDtypeStruct((rows, width), BF16),
            jax.ShapeDtypeStruct((8, 128), F32),
            jax.ShapeDtypeStruct(lanes, F32),
            jax.ShapeDtypeStruct(lanes, F32),
        ),
        in_specs=[hbm, hbm, vmem, vmem, vmem],
        out_specs=[hbm, hbm, vmem, vmem, vmem],
        scratch_shapes=[
            pltpu.VMEM((rows, width), BF16),
            pltpu.VMEM((rows, 1), F32),
            pltpu.VMEM((rows, width), BF16),
            pltpu.VMEM((width, rows), BF16),
            pltpu.VMEM((chips, 2, depth, states), BF16),
            pltpu.VMEM((rows, states), F32),
            pltpu.VMEM((rows, states), BF16),
            pltpu.VMEM((rows, width), F32),
            pltpu.VMEM((chips, 2, depth, states), BF16),
            pltpu.VMEM((chips, depth, states), BF16),
            pltpu.VMEM((len(slots), part, states), BF16),
            pltpu.VMEM((depth, states), BF16),
            pltpu.VMEM(lanes, BF16),
            pltpu.VMEM((groups - 1,) + lanes, BF16),
            pltpu.VMEM((8, 128), F32),
            pltpu.VMEM((n - 1, 8, 128), F32),
            pltpu.SemaphoreType.DMA((len(ids),)),
            pltpu.SemaphoreType.DMA((len(ids),)),
            pltpu.SemaphoreType.DMA((nsmall,)),
            pltpu.SemaphoreType.DMA((nsmall,)),
            pltpu.SemaphoreType.DMA((2,)),
        ],
        compiler_params=pltpu.CompilerParams(
            collective_id=0, has_side_effects=True, vmem_limit_bytes=63 * 2**20),
        cost_estimate=pl.CostEstimate(
            flops=flops, bytes_accessed=4 * rows * width, transcendentals=rows * states),
    )(frames.reshape(rows, width), out_weight, lab, chosen.reshape(lanes), previous.reshape(lanes))
    return (
        wg.reshape(1, depth, states),
        fg.reshape(micro, per, width),
        loss[0, :1],
        mom.reshape(entries),
        step.reshape(entries),
    )


def solution(mesh):
    return jax.shard_map(
        per_device,
        mesh=mesh,
        in_specs=(
            P(None, ("replica", "fsdp"), None),
            P("fsdp", None),
            P(None, ("replica", "fsdp")),
            P(None, ("replica", "fsdp")),
            P(None, "replica", "fsdp"),
            P(None, "fsdp"),
            P(),
        ),
        out_specs=(
            P("replica", "fsdp", None),
            P(None, ("replica", "fsdp"), None),
            P("replica"),
            P("fsdp"),
            P("fsdp"),
        ),
        check_vma=False,
    )
```

time: 212 us -> 152 us (0.72)
  Pallas kernels: 0 us -> 137 us
  waiting for transfers between devices: 117 us -> 0 us
  matrix products: 36.1 us -> 0 us
  other arithmetic: 20.4 us -> 0.75 us
  between operations: 18.8 us -> 1.31 us
  blocking collectives: 13.8 us -> 0 us
  local copies, waits for them, and re-layouts: 5.02 us -> 12.2 us
    pallas_call x0 -> x1, Pallas kernels: none -> 137 us  [per_device(): pl.pallas_call(functools.partial(kernel, n, groups, links, ids, slots), o...]
    all_gather x1 -> x0, waiting for transfers between devices: 67.1 us -> none  [per_device(): weight = lax.all_gather(out_weight, 'fsdp', axis=0, tiled=True)]
    reduce_scatter x1 -> x0, waiting for transfers between devices: 49.3 us -> none  [per_device(): lax.psum_scatter(lax.dot_general(normed_b, dlogits, (((0,), (0,)), ((), (...]
    dot_general x3 -> x0, matrix products: 36.1 us -> none  [the longest x1 14.9 us: per_device(): lax.dot_general(dlogits, weight, (((1,), (1,)), ((), ())), preferred_elem...]
    psum x1 -> x0, blocking collectives: 13.8 us -> none  [per_device(): total_loss = lax.psum(local_loss, 'fsdp')]
    convert_element_type x3 -> x0, other arithmetic: 8.89 us -> none  [the longest x1 5.84 us: per_device(): frame_grad = (inv_std * (dnormed - mean_grad - normed * mean_proj)).astyp...]
    reduce_sum x5 -> x0, other arithmetic: 7.77 us -> none  [the longest x1 3.13 us: per_device(): picked = jnp.sum(onehot * logp, axis=1)]
    dynamic_slice x0 -> x2, local copies, waits for them, and re-layouts: none -> 4.14 us  [the longest x1 2.47 us: per_device(): lax.dynamic_index_in_dim(momentum, fragment[0], 0, keepdims=False)]
  transfers between devices with their start and end apart: 3 -> 0, of which waited for: 2 -> 0; matrix products, arithmetic and copies ran while one was open for 28% -> 0% of each run, Pallas kernels for 0% -> 0%
where the time goes in v1:
time: 152 us; the launch traced here: 151 us
  Pallas kernels  137 us (90%)
  local copies, waits for them, and re-layouts  12.2 us (8%)
    pallas_call x1, Pallas kernels, per_device(): pl.pallas_call(functools.partial(kernel, n, groups, links, ids, slots), o...  137 us
    unnamed x12, local copies, waits for them, and re-layouts  6.71 us

profile of v1, /device:TPU:0, one launch (start us, length us, event | category | flops | bytes accessed | tf_op | source)
XLA Modules:
  0.0 151.3 jit_solution(11993260673212093424)
XLA Ops:
  1.3 0.8 fusion
  2.0 0.9 copy.14
  2.9 1.7 %constant_dynamic-slice_fusion.1 = f32[1,1,65536]{2,1,0:T(1,128)} fusion(f32[16,1,65536]{2,1,0:T(1,128)} %param.11, s32[]{:T(128)S(6)} %select_n.11), kind=kLoop, calls=%fused_computation.3 | loop fusion | bytes 524292 | tf_op jit(solution)/shard_map/jit(dynamic_index_in_dim)/dynamic_slice | solution.py:382
  4.6 2.5 %constant_dynamic-slice_fusion = f32[1,65536]{1,0:T(1,128)} fusion(f32[16,65536]{1,0:T(8,128)} %param.12, s32[]{:T(128)S(6)} %select_n.11), kind=kLoop, calls=%fused_computation.2 | loop fusion | bytes 524292 | tf_op jit(solution)/shard_map/jit(dynamic_index_in_dim)/dynamic_slice | solution.py:383
  7.0 137.0 %shard_map.110 = (bf16[384,2048]{1,0:T(8,128)(2,1)}, bf16[512,3072]{1,0:T(8,128)(2,1)}, f32[8,128]{1,0:T(8,128)}, f32[512,128]{1,0:T(8,128)}, f32[512,128]{1,0:T(8,128)}) custom-call(bf16[512,3072]{1,0:T(8,128)(2,1)} %bitcast.27, bf16[384,2048]{1,0:T(8,128)(2,1)} %w_hbm.1, s32[512,1]{1,0:T(8,128)} %bitcast.24, f32[512,128]{1,0:T(8,128)} %bitcast.20, ...), custom_call_target="tpu_custom_call" | custom-call | flops 19327352832 | bytes 6291456 | tf_op jit(solution)/shard_map/pallas_call | solution.py:398
  144.1 0.0 copy-start
  144.1 1.3 slice.3
  145.4 2.7 %copy.20 = bf16[1,384,2048]{2,1,0:T(8,128)(2,1)} copy(bf16[1,384,2048]{2,1,0:T(8,128)(2,1)} %bitcast.19) | data formatting | bytes 3145728
  148.1 0.0 copy-done
  148.2 0.0 copy-start.2
  148.2 0.0 copy-start.1
  148.2 1.7 %copy.21 = bf16[2,256,3072]{2,1,0:T(8,128)(2,1)} copy(bf16[2,256,3072]{2,1,0:T(8,128)(2,1)S(1)} %bitcast.18) | data formatting | bytes 6291456
  149.8 0.0 copy-done.2
  149.8 0.7 copy.22
  150.5 0.0 copy-done.1
  150.5 0.7 copy.23
  (1 shorter events, 0.0 us)
Async XLA Ops:
  144.1 4.1 %copy-start = (bf16[512,3072]{1,0:T(8,128)(2,1)S(1)}, bf16[512,3072]{1,0:T(8,128)(2,1)}, u32[]{:S(2)}) copy-start(bf16[512,3072]{1,0:T(8,128)(2,1)} %get-tuple-element.11) | copy-start | bytes 9437188
  148.2 1.7 %copy-start.2 = (f32[512,128]{1,0:T(8,128)S(1)}, f32[512,128]{1,0:T(8,128)}, u32[]{:S(2)}) copy-start(f32[512,128]{1,0:T(8,128)} %get-tuple-element.13) | copy-start | bytes 786436
  148.2 2.4 %copy-start.1 = (f32[512,128]{1,0:T(8,128)S(1)}, f32[512,128]{1,0:T(8,128)}, u32[]{:S(2)}) copy-start(f32[512,128]{1,0:T(8,128)} %get-tuple-element.14) | copy-start | bytes 786436

commit v2 on v1

--- a/solution.py
+++ b/solution.py
@@ -26,7 +26,13 @@
     return bin(value).count("1")
 
 
-def plan(links):
+def pieces(depth, links):
+    subs = links if depth % (48 * links) == 0 else 1
+    size = depth // (3 * subs)
+    return [(third, i, (third + i) % links if subs == 1 else i, size) for third in range(3) for i in range(subs)]
+
+
+def plan(links, depth):
     chips = 2**links
     ids = {}
 
@@ -34,10 +40,10 @@
         ids[key] = len(ids)
 
     new(("own_core",))
-    for p in range(links):
+    for g in range(len(pieces(depth, links))):
         for m in range(1, chips):
-            new(("gather", p, m))
-            new(("gather_core", p, m))
+            new(("gather", g, m))
+            new(("gather_core", g, m))
     for m in range(chips):
         new(("term_core", m))
     for p in range(links):
@@ -54,7 +60,7 @@
 
 def kernel(n, groups, links, ids, slots, frames_hbm, w_hbm, lab_ref, mine_ref, prev_ref,
            wg_hbm, fg_hbm, loss_ref, mom_ref, step_ref,
-           fbuf, inv_ref, nb, nbt, wbuf, logits, dl, dn, tb, crecv, rx, wgbuf,
+           fbuf, inv_ref, nb, nbt, wbuf, logits, dl, dn, tb, crecv, rx,
            dsend, drecv, losssend, lossrecv,
            send, recv, small_send, small_recv, local):
     me = lax.axis_index("fsdp")
@@ -102,18 +108,33 @@
     def span(p):
         return pl.ds(p * part, part)
 
-    def gather_copy(p, s, m):
-        bit = order(links, p)[s]
-        src = w_hbm.at[span(p)] if m == 0 else wbuf.at[m, core, span(p)]
-        return rdma(("gather", p, m | bit), src, wbuf.at[m | bit, core, span(p)], peer(bit))
-
-    def gather_core_copy(p, m):
-        return rdma(("gather_core", p, m), wbuf.at[m, core, span(p)],
-                    wbuf.at[m, core, span(p)], sibling)
-
-    for s in range(links):
-        for p in range(links):
-            go(gather_copy(p, s, 0))
+    cuts = pieces(depth, links)
+    subs = len(cuts) // 3
+    parity = group % 2
+    partner = {"replica": flip(group, 1)}
+
+    def cut(g):
+        third, i, _, size = cuts[g]
+        place = third + parity * (2 - 2 * third)
+        return pl.ds(pl.multiple_of((place * subs + i) * size, size), size)
+
+    def gather_copy(g, s, m):
+        bit = order(links, cuts[g][2])[s]
+        src = w_hbm.at[cut(g)] if m == 0 else wbuf.at[m, core, cut(g)]
+        return rdma(("gather", g, m | bit), src, wbuf.at[m | bit, core, cut(g)], peer(bit))
+
+    def gather_core_copy(g, m):
+        return rdma(("gather_core", g, m), wbuf.at[m, core, cut(g)],
+                    wbuf.at[m, core, cut(g)], sibling)
+
+    def partner_copy(g, m):
+        return rdma(("gather", g + 2 * subs, m), wbuf.at[m, core, cut(g)],
+                    wbuf.at[m, core, cut(g)], partner)
+
+    for third in range(2):
+        for s in range(links):
+            for g in range(third * subs, (third + 1) * subs):
+                go(gather_copy(g, s, 0))
     own_core = rdma(("own_core",), w_hbm, wbuf.at[0, core], sibling)
     go(own_core)
 
@@ -140,7 +161,7 @@
         inv_ref[r, :] = inv
         return carry
 
-    lax.fori_loop(0, rows // tile, norm_tile, 0)
+    lax.fori_loop(0, rows // tile, norm_tile, 0, unroll=2)
 
     def transpose_tile(i, carry):
         c = pl.ds(pl.multiple_of(i * ntile, ntile), ntile)
@@ -163,46 +184,49 @@
                 logits[:, c] += out
             return carry
 
-        lax.fori_loop(0, states // ntile, body, 0)
+        lax.fori_loop(0, states // ntile, body, 0, unroll=2)
 
     arrivals = []
-    for m in range(1, chips):
-        for p in range(links):
-            bits = order(links, p)
+    ranks = sorted({(popcount(m), max(s for s in range(links) if m & order(links, 0)[s])) for m in range(1, chips)})
+    for g, (third, _, path, _) in enumerate(cuts):
+        bits = order(links, path)
+        for m in range(1, chips):
             last = max(s for s in range(links) if m & bits[s])
-            arrivals.append((popcount(m), last, p, m))
+            rank = ranks.index((popcount(m), last))
+            arrivals.append((rank + (0, len(ranks), len(ranks) + 0.5)[third], g, last, m))
     arrivals.sort()
 
-    def arrive(last, p, m):
-        bits = order(links, p)
-        gather_copy(p, last, m & ~bits[last]).wait_recv()
-        for s in range(last + 1, links):
-            go(gather_copy(p, s, m))
-        go(gather_core_copy(p, m))
+    def arrive(g, last, m):
+        third, _, path, _ = cuts[g]
+        bits = order(links, path)
+        if third == 2:
+            partner_copy(g - 2 * subs, m).wait_recv()
+        else:
+            gather_copy(g, last, m & ~bits[last]).wait_recv()
+            for s in range(last + 1, links):
+                go(gather_copy(g, s, m))
+        if third == 0:
+            go(partner_copy(g, m))
+        go(gather_core_copy(g, m))
 
     done = set()
-    logged = [False]
-
-    def ready_dots():
-        for m in range(1, chips):
-            if m not in done and all((p, m) in seen for p in range(links)):
-                done.add(m)
-                for p in range(links):
-                    gather_core_copy(p, m).wait_recv()
-                logits_chip(m, False)
-
     seen = set()
-    for index, (_, last, p, m) in enumerate(arrivals):
-        arrive(last, p, m)
-        seen.add((p, m))
-        if index == links - 1:
+    for index, (_, g, last, m) in enumerate(arrivals):
+        arrive(g, last, m)
+        seen.add((g, m))
+        if index == subs - 1:
             lax.fori_loop(0, width // ntile, transpose_tile, 0)
+        if index == 2 * subs - 1:
             own_in.wait()
             own_core.wait_recv()
             logits_chip(0, True)
-        if index >= links - 1 and (index + 1) % links == 0:
-            ready_dots()
-    ready_dots()
+        if index + 1 == len(arrivals) or arrivals[index + 1][0] != arrivals[index][0]:
+            for m in range(1, chips):
+                if m not in done and all((g, m) in seen for g in range(len(cuts))):
+                    done.add(m)
+                    for g in range(len(cuts)):
+                        gather_core_copy(g, m).wait_recv()
+                    logits_chip(m, False)
 
     def softmax_tile(i, total):
         r = pl.ds(pl.multiple_of(i * tile, tile), tile)
@@ -219,7 +243,7 @@
         dl[r, :] = jnp.where(hit, d - 1.0, d).astype(BF16)
         return total + valid * (top + jnp.log(norm) - picked)
 
-    total = lax.fori_loop(0, rows // tile, softmax_tile, jnp.zeros((tile, 1), F32))
+    total = lax.fori_loop(0, rows // tile, softmax_tile, jnp.zeros((tile, 1), F32), unroll=2)
 
     slot_of = slots
 
@@ -232,7 +256,7 @@
             tb[m, :, :, c] = out.reshape(2, depth, ntile)
             return carry
 
-        lax.fori_loop(0, states // ntile, body, 0)
+        lax.fori_loop(0, states // ntile, body, 0, unroll=2)
 
     def term_copy(m):
         return rdma(("term_core", m), tb.at[m, other], crecv.at[m], sibling)
@@ -251,7 +275,7 @@
             tb[m, core, r, :] = (tb[m, core, r, :].astype(F32) + crecv[m, r, :].astype(F32)).astype(BF16)
             return carry
 
-        lax.fori_loop(0, depth // add_tile, body, 0)
+        lax.fori_loop(0, depth // add_tile, body, 0, unroll=2)
 
     def finish_core(m):
         term_copy(m).wait_recv()
@@ -300,13 +324,10 @@
             value = tb[m, core, here, :].astype(F32)
             for t in range(s):
                 value = value + rx[slot_of[(p, t, m)], pl.ds(r, add_tile), :].astype(F32)
-            if m == 0:
-                wgbuf[here, :] = value.astype(BF16)
-            else:
-                tb[m, core, here, :] = value.astype(BF16)
+            tb[m, core, here, :] = value.astype(BF16)
             return carry
 
-        lax.fori_loop(0, part // add_tile, body, 0)
+        lax.fori_loop(0, part // add_tile, body, 0, unroll=2)
 
     def reduce_wait(p, s, m):
         bit = order(links, p)[s]
@@ -338,7 +359,7 @@
         fbuf[r, :] = (inv_ref[r, :] * (d - mean_grad - x * mean_proj)).astype(BF16)
         return carry
 
-    lax.fori_loop(0, rows // tile, grad_tile, 0)
+    lax.fori_loop(0, rows // tile, grad_tile, 0, unroll=2)
     frames_out = pltpu.make_async_copy(fbuf, fg_hbm, local.at[0])
     frames_out.start()
 
@@ -362,7 +383,7 @@
     for p in range(links):
         need(p, links, 0)
         add_received(p, links, 0)
-    grad_out = pltpu.make_async_copy(wgbuf, wg_hbm, local.at[1])
+    grad_out = pltpu.make_async_copy(tb.at[0, core], wg_hbm, local.at[1])
     grad_out.start()
     for copy in started + small + losses:
         copy.wait_send()
@@ -386,7 +407,7 @@
     position = jnp.arange(per, dtype=jnp.int32)
     lab = jnp.where(position[None, :] < lengths, align, -1).reshape(rows, 1)
 
-    ids = plan(links)
+    ids = plan(links, depth)
     slots = {}
     for key in ids:
         if key[0] == "reduce":
@@ -418,7 +439,6 @@
             pltpu.VMEM((chips, 2, depth, states), BF16),
             pltpu.VMEM((chips, depth, states), BF16),
             pltpu.VMEM((len(slots), part, states), BF16),
-            pltpu.VMEM((depth, states), BF16),
             pltpu.VMEM(lanes, BF16),
             pltpu.VMEM((groups - 1,) + lanes, BF16),
             pltpu.VMEM((8, 128), F32),

time: 152 us -> 136 us (0.89)
  Pallas kernels: 137 us -> 121 us
    pallas_call x1, Pallas kernels: 137 us -> 121 us  [per_device(): pl.pallas_call(functools.partial(kernel, n, groups, links, ids, slots), o...]
where the time goes in v2:
time: 136 us
  Pallas kernels  121 us (89%)
  local copies, waits for them, and re-layouts  12.2 us (9%)
    pallas_call x1, Pallas kernels, per_device(): pl.pallas_call(functools.partial(kernel, n, groups, links, ids, slots), o...  121 us
    unnamed x12, local copies, waits for them, and re-layouts  6.71 us

profile of v2, /device:TPU:0, one launch (start us, length us, event | category | flops | bytes accessed | tf_op | source)
XLA Modules:
  0.0 135.7 jit_solution(9388204034069050420)
XLA Ops:
  1.3 0.8 fusion
  2.0 0.9 copy.14
  2.9 1.7 %constant_dynamic-slice_fusion.1 = f32[1,1,65536]{2,1,0:T(1,128)} fusion(f32[16,1,65536]{2,1,0:T(1,128)} %param.11, s32[]{:T(128)S(6)} %select_n.11), kind=kLoop, calls=%fused_computation.3 | loop fusion | bytes 524292 | tf_op jit(solution)/shard_map/jit(dynamic_index_in_dim)/dynamic_slice | solution.py:403
  4.6 2.5 %constant_dynamic-slice_fusion = f32[1,65536]{1,0:T(1,128)} fusion(f32[16,65536]{1,0:T(8,128)} %param.12, s32[]{:T(128)S(6)} %select_n.11), kind=kLoop, calls=%fused_computation.2 | loop fusion | bytes 524292 | tf_op jit(solution)/shard_map/jit(dynamic_index_in_dim)/dynamic_slice | solution.py:404
  7.0 121.4 %shard_map.110 = (bf16[384,2048]{1,0:T(8,128)(2,1)}, bf16[512,3072]{1,0:T(8,128)(2,1)}, f32[8,128]{1,0:T(8,128)}, f32[512,128]{1,0:T(8,128)}, f32[512,128]{1,0:T(8,128)}) custom-call(bf16[512,3072]{1,0:T(8,128)(2,1)} %bitcast.27, bf16[384,2048]{1,0:T(8,128)(2,1)} %w_hbm.1, s32[512,1]{1,0:T(8,128)} %bitcast.24, f32[512,128]{1,0:T(8,128)} %bitcast.20, ...), custom_call_target="tpu_custom_call" | custom-call | flops 19327352832 | bytes 6291456 | tf_op jit(solution)/shard_map/pallas_call | solution.py:419
  128.5 0.0 copy-start
  128.5 1.3 slice.3
  129.8 2.7 %copy.20 = bf16[1,384,2048]{2,1,0:T(8,128)(2,1)} copy(bf16[1,384,2048]{2,1,0:T(8,128)(2,1)} %bitcast.19) | data formatting | bytes 3145728
  132.6 0.0 copy-done
  132.6 0.0 copy-start.2
  132.6 0.0 copy-start.1
  132.6 1.7 %copy.21 = bf16[2,256,3072]{2,1,0:T(8,128)(2,1)} copy(bf16[2,256,3072]{2,1,0:T(8,128)(2,1)S(1)} %bitcast.18) | data formatting | bytes 6291456
  134.2 0.0 copy-done.2
  134.2 0.7 copy.22
  135.0 0.0 copy-done.1
  135.0 0.7 copy.23
  (1 shorter events, 0.0 us)
Async XLA Ops:
  128.5 4.1 %copy-start = (bf16[512,3072]{1,0:T(8,128)(2,1)S(1)}, bf16[512,3072]{1,0:T(8,128)(2,1)}, u32[]{:S(2)}) copy-start(bf16[512,3072]{1,0:T(8,128)(2,1)} %get-tuple-element.11) | copy-start | bytes 9437188
  132.6 1.7 %copy-start.2 = (f32[512,128]{1,0:T(8,128)S(1)}, f32[512,128]{1,0:T(8,128)}, u32[]{:S(2)}) copy-start(f32[512,128]{1,0:T(8,128)} %get-tuple-element.13) | copy-start | bytes 786436
  132.6 2.4 %copy-start.1 = (f32[512,128]{1,0:T(8,128)S(1)}, f32[512,128]{1,0:T(8,128)}, u32[]{:S(2)}) copy-start(f32[512,128]{1,0:T(8,128)} %get-tuple-element.14) | copy-start | bytes 786436
